TPU v7x, 32 devices: a whole 2x2x4 slice. The times are simulated.
32 devices in a mesh: groups: 2 (over y), gx: 4 (over z), gy: 4 (over x, core).
Axes of the slice: x: 2, y: 2, z: 4, core: 2. Of those that a mesh axis runs over, the one named last changes fastest.
Arguments:
- tokens: bfloat16 [2, 384, 8192], P(None, ('groups', 'gy'), 'gx'), parts along dimension 1, may hold values from -6 to 6
- gate_weight: bfloat16 [8192, 26624], P('gx', 'gy'), may hold values from -0.0625 to 0.0625
- up_weight: bfloat16 [8192, 26624], P('gx', 'gy'), may hold values from -0.0625 to 0.0625
- gate_scale: float32 [26624], P('gy'), may hold values from 0.3 to 3
- up_scale: float32 [26624], P('gy'), may hold values from 0.3 to 3
- down_weight: bfloat16 [26624, 8192], P('gy', 'gx'), may hold values from -0.0390625 to 0.0390625
- down_scale: float32 [8192], P('gx'), may hold values from 0.3 to 3
Outputs:
- mixed: bfloat16 [2, 384, 8192], P(None, ('groups', 'gy'), 'gx'), parts along dimension 1
There are 2 independent parts, one for each index of `groups`. A program takes and returns all parts, laid end to end along the dimension named above; an argument that names none is the same for every part. Nothing has to cross between parts.
All inputs are finite; a program needn't handle non-finite values.
Results may differ from a plain program's by a relative error of at most 0.028.
Values may be sent and summed in bfloat16 or wider, within the bound.
No kernel may reach another device: no remote copies, remote signals or barrier semaphores. Data moves between devices by JAX's collectives and lax.ppermute only.
A program may use at most 256 MiB of HBM per device.

v0:
```python
import jax
import jax.numpy as jnp
from jax import lax
from jax.sharding import PartitionSpec as P


def activate(sums, gate_scale, up_scale):
    gate = sums[0] * gate_scale
    up = sums[1] * up_scale
    return (jax.nn.silu(gate) * up).astype(jnp.bfloat16)


def block(rows_in, gate_weight, up_weight, gate_scale, up_scale, down_weight, down_scale):
    piece = lax.all_gather(rows_in, "gy", axis=1, tiled=True)
    gate_term = jnp.einsum("snd,df->snf", piece, gate_weight, preferred_element_type=jnp.float32)
    up_term = jnp.einsum("snd,df->snf", piece, up_weight, preferred_element_type=jnp.float32)
    partial_terms = jnp.stack([gate_term, up_term], axis=0)
    sums = lax.psum(partial_terms.astype(jnp.bfloat16), "gx").astype(jnp.float32)
    hidden = activate(sums, gate_scale, up_scale)
    down_term = jnp.einsum("srf,fd->srd", hidden, down_weight, preferred_element_type=jnp.float32)
    down_sum = lax.psum_scatter(
        down_term.astype(jnp.bfloat16), "gy", scatter_dimension=1, tiled=True
    ).astype(jnp.float32)
    return (down_sum * down_scale).astype(jnp.bfloat16)


def per_device(tokens, gate_weight, up_weight, gate_scale, up_scale, down_weight, down_scale):
    results = []
    for step in range(tokens.shape[0]):
        results.append(
            block(
                tokens[step : step + 1],
                gate_weight,
                up_weight,
                gate_scale,
                up_scale,
                down_weight,
                down_scale,
            )
        )
    return jnp.concatenate(results, axis=0)


def solution(mesh):
    placed = (
        P(None, ("groups", "gy"), "gx"),
        P("gx", "gy"),
        P("gx", "gy"),
        P("gy"),
        P("gy"),
        P("gy", "gx"),
        P("gx"),
    )
    return jax.shard_map(
        per_device,
        mesh=mesh,
        in_specs=placed,
        out_specs=P(None, ("groups", "gy"), "gx"),
        check_vma=False,
    )
```

profile of v0, /device:TPU:0, one launch (start us, length us, event | category | flops | bytes accessed | tf_op | source)
XLA Modules:
  0.0 514.6 jit_solution(10796694603755923438)
XLA Ops:
  6.5 0.0 all-reduce.3.cloned.1.call-start
  6.5 1.0 fusion.40
  7.6 10.0 %all_gather.6 = bf16[1,192,2048]{2,1,0:T(8,128)(2,1)S(1)} all-gather(bf16[1,48,2048]{2,1,0:T(8,128)(2,1)S(1)} %get-tuple-element.7), channel_id=1, replica_groups=mesh['groups'=2,'gx'=4,'gy'=4] {'gy'}, dimensions={1}, use_global_device_ids=true | all-gather | bytes 983040 | tf_op jit(solution)/shard_map/all_gather | solution.py:14
  17.6 8.7 %all_gather.7 = bf16[1,192,2048]{2,1,0:T(8,128)(2,1)S(1)} all-gather(bf16[1,48,2048]{2,1,0:T(8,128)(2,1)S(1)} %get-tuple-element.8), channel_id=1, replica_groups=mesh['groups'=2,'gx'=4,'gy'=4] {'gy'}, dimensions={1}, use_global_device_ids=true | all-gather | bytes 983040 | tf_op jit(solution)/shard_map/all_gather | solution.py:14
  26.3 11.8 %fusion.3 = bf16[1,1,192,6656]{3,2,1,0:T(8,128)(2,1)S(1)} fusion(bf16[2048,6656]{1,0:T(8,128)(2,1)} %param.9, bf16[1,192,2048]{2,1,0:T(8,128)(2,1)S(1)} %all_gather.7), kind=kOutput, calls=%fused_computation.7 | convolution fusion | flops 5235769344 | bytes 30605312 | tf_op jit(solution)/shard_map/snd,df->snf/dot_general | solution.py:16
  38.2 11.8 %fusion.2 = bf16[1,1,192,6656]{3,2,1,0:T(8,128)(2,1)S(1)} fusion(bf16[2048,6656]{1,0:T(8,128)(2,1)} %param.8, bf16[1,192,2048]{2,1,0:T(8,128)(2,1)S(1)} %all_gather.7), kind=kOutput, calls=%fused_computation.6 | convolution fusion | flops 5235769344 | bytes 30605312 | tf_op jit(solution)/shard_map/snd,df->snf/dot_general | solution.py:15
  50.0 11.8 %fusion.1 = bf16[1,1,192,6656]{3,2,1,0:T(8,128)(2,1)S(1)} fusion(bf16[2048,6656]{1,0:T(8,128)(2,1)} %param.9, bf16[1,192,2048]{2,1,0:T(8,128)(2,1)S(1)} %all_gather.6), kind=kOutput, calls=%fused_computation.5 | convolution fusion | flops 5235769344 | bytes 30605312 | tf_op jit(solution)/shard_map/snd,df->snf/dot_general | solution.py:16
  61.9 11.8 %fusion = bf16[1,1,192,6656]{3,2,1,0:T(8,128)(2,1)S(1)} fusion(bf16[2048,6656]{1,0:T(8,128)(2,1)} %param.8, bf16[1,192,2048]{2,1,0:T(8,128)(2,1)S(1)} %all_gather.6), kind=kOutput, calls=%fused_computation.4 | convolution fusion | flops 5235769344 | bytes 30605312 | tf_op jit(solution)/shard_map/snd,df->snf/dot_general | solution.py:15
  73.7 2.7 pad_maximum_fusion.1
  76.5 2.7 pad_maximum_fusion
  79.2 0.0 all-reduce.3.cloned.1.call-update
  79.2 0.2 reduce-scatter.5.cloned.1.call-start
  79.4 351.5 %all-reduce.3.cloned.1.call-done = (bf16[2,1,192,6656]{3,2,1,0:T(8,128)(2,1)}, bf16[2,1,192,6656]{3,2,1,0:T(8,128)(2,1)}) async-done(((bf16[2,1,192,6656]{3,2,1,0:T(8,128)(2,1)}, bf16[2,1,192,6656]{3,2,1,0:T(8,128)(2,1)}), (bf16[2,1,192,6656]{3,2,1,0:T(8,128)(2,1)}, bf16[2,1,192,6656]{3,2,1,0:T(8,128)(2,1)})) %all-reduce.3.cloned.1.call-update) | async-done | bytes 10223632 | tf_op jit(solution)/shard_map/psum | solution.py:18
  431.0 0.0 copy-start.1
  431.0 0.0 copy-start.2
  431.0 7.6 %convert_element_type.66 = f32[2,1,192,6656]{3,2,1,0:T(8,128)} convert(bf16[2,1,192,6656]{3,2,1,0:T(8,128)(2,1)} %get-tuple-element.5) | non-fusion elementwise | flops 2555904 | bytes 15335424 | tf_op jit(solution)/shard_map/convert_element_type | solution.py:18
  438.6 0.0 copy-done.1
  438.6 0.0 copy-done.2
  438.6 18.6 %fusion.31 = bf16[1,192,2048]{2,1,0:T(8,128)(2,1)} fusion(bf16[6656,2048]{1,0:T(8,128)(2,1)} %param.12, f32[2,1,192,6656]{3,2,1,0:T(8,128)} %convert_element_type.66, f32[6656]{0:T(1024)S(1)} %copy-done.1, f32[6656]{0:T(1024)S(1)} %copy-done.2), kind=kOutput, calls=%fused_computation.33 | convolution fusion | flops 5245108224 | bytes 38326272 | tf_op jit(solution)/shard_map/srf,fd->srd/dot_general | solution.py:20
  457.2 0.0 reduce-scatter.5.cloned.1.call-update
  457.2 0.0 reduce-scatter.3.cloned.1.call-start
  457.3 7.6 %convert_element_type.60 = f32[2,1,192,6656]{3,2,1,0:T(8,128)} convert(bf16[2,1,192,6656]{3,2,1,0:T(8,128)(2,1)} %get-tuple-element.6) | non-fusion elementwise | flops 2555904 | bytes 15335424 | tf_op jit(solution)/shard_map/convert_element_type | solution.py:18
  464.9 0.0 copy-start
  464.9 18.8 %fusion.28 = bf16[1,192,2048]{2,1,0:T(8,128)(2,1)} fusion(bf16[6656,2048]{1,0:T(8,128)(2,1)} %param.12, f32[2,1,192,6656]{3,2,1,0:T(8,128)} %convert_element_type.60, f32[6656]{0:T(1024)S(1)} %copy-done.1, f32[6656]{0:T(1024)S(1)} %copy-done.2), kind=kOutput, calls=%fused_computation.32 | convolution fusion | flops 5245108224 | bytes 38326272 | tf_op jit(solution)/shard_map/srf,fd->srd/dot_general | solution.py:20
  483.6 0.0 reduce-scatter.3.cloned.1.call-update
  483.7 0.0 reduce-scatter.5.cloned.1.call-done
  483.7 22.5 %reduce-scatter.3.cloned.1.call-done = bf16[1,48,2048]{2,1,0:T(8,128)(2,1)} async-done(((bf16[1,192,2048]{2,1,0:T(8,128)(2,1)}), bf16[1,48,2048]{2,1,0:T(8,128)(2,1)}) %reduce-scatter.3.cloned.1.call-update) | async-done | bytes 196624 | tf_op jit(solution)/shard_map/reduce_scatter | solution.py:21
  506.2 0.0 copy-done
  506.2 1.1 multiply_convert_fusion.1
  507.3 0.8 pad_maximum_fusion.2
Async XLA Ops:
  6.5 424.4 %all-reduce.3.cloned.1.call-start = ((), (), s32[]{:S(2)}) async-start(), calls=%async_computation.4 | async-start | bytes 20447232 | tf_op jit(solution)/shard_map/psum | solution.py:18
  79.2 404.5 %reduce-scatter.5.cloned.1.call-start = ((), (), s32[]{:S(2)}) async-start(), calls=%async_computation.3 | async-start | bytes 983040 | tf_op jit(solution)/shard_map/reduce_scatter | solution.py:21
  431.0 7.6 %copy-start.1 = (f32[6656]{0:T(1024)S(1)}, f32[6656]{0:T(1024)}, u32[]{:S(2)}) copy-start(f32[6656]{0:T(1024)} %param.11) | copy-start | bytes 79876
  431.0 7.6 %copy-start.2 = (f32[6656]{0:T(1024)S(1)}, f32[6656]{0:T(1024)}, u32[]{:S(2)}) copy-start(f32[6656]{0:T(1024)} %param.10) | copy-start | bytes 79876
  457.2 48.9 %reduce-scatter.3.cloned.1.call-start = ((), (), s32[]{:S(2)}) async-start(), calls=%async_computation.2 | async-start | bytes 983040 | tf_op jit(solution)/shard_map/reduce_scatter | solution.py:21
  464.9 41.3 %copy-start = (f32[2048]{0:T(1024)S(1)}, f32[2048]{0:T(1024)}, u32[]{:S(2)}) copy-start(f32[2048]{0:T(1024)} %param.13) | copy-start | bytes 24580
Sparse Core Ops, SparseCore 0:
  79.3 351.6 all-reduce.2
  457.3 22.2 reduce-scatter.4
  483.8 22.3 reduce-scatter.2
where the time goes:
time: 515 us
  waiting for transfers between devices  374 us (73%)
  matrix products  84.7 us (16%)
  other arithmetic  22.5 us (4%)
  blocking collectives  18.8 us (4%)
  between operations  13.2 us (3%)
    psum x1, waiting for transfers between devices, block(): lax.psum(partial_terms.astype(jnp.bfloat16), 'gx').astype(jnp.float32)  352 us
    dot_general x2, matrix products, block(): jnp.einsum('srf,fd->srd', hidden, down_weight, preferred_element_type=jnp...  37.3 us
    dot_general x2, matrix products, block(): jnp.einsum('snd,df->snf', piece, gate_weight, preferred_element_type=jnp....  23.7 us
    dot_general x2, matrix products, block(): jnp.einsum('snd,df->snf', piece, up_weight, preferred_element_type=jnp.fl...  23.7 us
    reduce_scatter x2, waiting for transfers between devices, block(): lax.psum_scatter(down_term.astype(jnp.bfloat16), 'gy', scatter_dimension=...  22.5 us
    all_gather x2, blocking collectives, block(): piece = lax.all_gather(rows_in, 'gy', axis=1, tiled=True)  18.8 us
    convert_element_type x2, other arithmetic, block(): lax.psum(partial_terms.astype(jnp.bfloat16), 'gx').astype(jnp.float32)  15.2 us
  transfers between devices with their start and end apart: 3, of which 2 were waited for; matrix products, arithmetic and copies ran while one was open for 5% of the time, Pallas kernels for 0%

commit v1 on v0

v1 whole, which is shorter than its diff:
```python
import functools

import jax
import jax.numpy as jnp
from jax import lax
from jax.experimental import pallas as pl
from jax.experimental.pallas import tpu as pltpu
from jax.sharding import PartitionSpec as P

VMEM = 48 * 1024 * 1024


def width_of(units):
    return max(w for w in range(128, 513, 128) if units % w == 0)


def tile_of(size, limit):
    return max(t for t in range(128, min(size, limit) + 1, 128) if size % t == 0)


def params(**more):
    return pltpu.CompilerParams(vmem_limit_bytes=VMEM, **more)


def project(place, rows, gate_weight, up_weight, step, width):
    count, depth = rows.shape
    chunks = gate_weight.shape[1] // width
    tile = tile_of(width, 256)
    tiles = width // tile

    def kernel(place_ref, rows_ref, gate_ref, up_ref, out_ref):
        x = rows_ref[...]
        out_ref[0] = jnp.dot(x, gate_ref[...], preferred_element_type=jnp.float32).astype(jnp.bfloat16)
        out_ref[1] = jnp.dot(x, up_ref[...], preferred_element_type=jnp.float32).astype(jnp.bfloat16)

    def weight(j, place_ref):
        return 0, jnp.clip(step - place_ref[0], 0, chunks - 1) * tiles + j

    return pl.pallas_call(
        kernel,
        grid_spec=pltpu.PrefetchScalarGridSpec(
            num_scalar_prefetch=1,
            grid=(tiles,),
            in_specs=[
                pl.BlockSpec((count, depth), lambda j, place_ref: (0, 0)),
                pl.BlockSpec((depth, tile), weight),
                pl.BlockSpec((depth, tile), weight),
            ],
            out_specs=pl.BlockSpec((2, count, tile), lambda j, place_ref: (0, 0, j)),
        ),
        out_shape=jax.ShapeDtypeStruct((2, count, width), jnp.bfloat16),
        compiler_params=params(),
        name="project",
    )(place, rows, gate_weight, up_weight)


def combine(place, part, received, scales, step, last):
    _, count, width = part.shape
    chunks = scales.shape[0]
    rows = count // 3 if count % 48 == 0 else count

    def kernel(place_ref, part_ref, recv_ref, scale_ref, sum_ref, hidden_ref):
        gate = part_ref[0].astype(jnp.float32) + recv_ref[0].astype(jnp.float32)
        up = part_ref[1].astype(jnp.float32) + recv_ref[1].astype(jnp.float32)

        @pl.when(place_ref[0] != last)
        def _():
            sum_ref[0] = gate.astype(jnp.bfloat16)
            sum_ref[1] = up.astype(jnp.bfloat16)

        @pl.when(place_ref[0] == last)
        def _():
            g = gate * scale_ref[0, 0:1, :]
            u = up * scale_ref[0, 1:2, :]
            hidden_ref[...] = (jax.nn.silu(g) * u).astype(jnp.bfloat16)

    def scale(i, place_ref):
        return jnp.clip(step - place_ref[0], 0, chunks - 1), 0, 0

    block = pl.BlockSpec((2, rows, width), lambda i, place_ref: (0, i, 0))
    return pl.pallas_call(
        kernel,
        grid_spec=pltpu.PrefetchScalarGridSpec(
            num_scalar_prefetch=1,
            grid=(count // rows,),
            in_specs=[block, block, pl.BlockSpec((1, 2, width), scale)],
            out_specs=[block, pl.BlockSpec((rows, width), lambda i, place_ref: (i, 0))],
        ),
        out_shape=[
            jax.ShapeDtypeStruct(part.shape, jnp.bfloat16),
            jax.ShapeDtypeStruct((count, width), jnp.bfloat16),
        ],
        compiler_params=params(),
        name="combine",
    )(place, part, received, scales)


def reduce_down(place, hidden, received, down_weight, total, step, last):
    count, width = hidden.shape
    outs = down_weight.shape[1]
    chunks = down_weight.shape[0] // width
    tile = tile_of(outs, 512)

    def kernel(place_ref, hidden_ref, recv_ref, weight_ref, *rest):
        total_ref = rest[0] if total is not None else None
        send_ref, out_ref = rest[-2:]

        @pl.when(pl.program_id(0) == 0)
        def _():
            @pl.when(place_ref[0] == last)
            def _():
                send_ref[...] = hidden_ref[...]

            @pl.when(place_ref[0] != last)
            def _():
                send_ref[...] = recv_ref[...]

        chunk = step - 2 * last + place_ref[0]
        valid = jnp.logical_and(chunk >= 0, chunk < chunks)

        @pl.when(valid)
        def _():
            term = jnp.dot(send_ref[...], weight_ref[...], preferred_element_type=jnp.float32)
            out_ref[...] = term if total_ref is None else total_ref[...] + term

        @pl.when(jnp.logical_not(valid))
        def _():
            out_ref[...] = jnp.zeros_like(out_ref) if total_ref is None else total_ref[...]

    def weight(j, place_ref):
        return jnp.clip(step - 2 * last + place_ref[0], 0, chunks - 1), j

    whole = pl.BlockSpec((count, width), lambda j, place_ref: (0, 0))
    part = pl.BlockSpec((count, tile), lambda j, place_ref: (0, j))
    more = [] if total is None else [total]
    return pl.pallas_call(
        kernel,
        grid_spec=pltpu.PrefetchScalarGridSpec(
            num_scalar_prefetch=1,
            grid=(outs // tile,),
            in_specs=[whole, whole, pl.BlockSpec((width, tile), weight)] + [part] * len(more),
            out_specs=[whole, part],
        ),
        out_shape=[
            jax.ShapeDtypeStruct((count, width), jnp.bfloat16),
            jax.ShapeDtypeStruct((count, outs), jnp.float32),
        ],
        input_output_aliases={4: 1} if more else {},
        compiler_params=params(),
        name="reduce_down",
    )(place, hidden, received, down_weight, *more)


def per_device(mesh, tokens, gate_weight, up_weight, gate_scale, up_scale, down_weight, down_scale):
    n_gx, n_gy = mesh.shape["gx"], mesh.shape["gy"]
    last = n_gx - 1
    towards, back = [], []
    for z in range(n_gx):
        for g in range(n_gy):
            to = z - 1 if g % 2 == 0 else z + 1
            if 0 <= to < n_gx:
                towards.append((z * n_gy + g, to * n_gy + g))
                back.append((to * n_gy + g, z * n_gy + g))
    z, g = lax.axis_index("gx"), lax.axis_index("gy")
    place = jnp.where(g % 2 == 0, last - z, z).astype(jnp.int32).reshape(1)

    units = gate_weight.shape[1]
    width = width_of(units)
    chunks = units // width
    scales = jnp.stack([gate_scale.reshape(chunks, width), up_scale.reshape(chunks, width)], axis=1)

    rows = lax.all_gather(tokens, "gy", axis=1, tiled=True)
    steps, count, depth = rows.shape
    rows = rows.reshape(steps * count, depth)

    send, hidden, total, passed = None, None, None, None
    for step in range(chunks + 2 * last):
        summing = step < chunks + last
        if summing:
            part = project(place, rows, gate_weight, up_weight, step, width)
            if step == 0:
                got = jnp.zeros_like(part)
            else:
                got = lax.ppermute(send, ("gx", "gy"), towards)
            send, hidden = combine(place, part, got, scales, step, last)
        if step >= last:
            if step == last:
                held = jnp.zeros_like(hidden)
            else:
                held = lax.ppermute(passed, ("gx", "gy"), back)
            passed, total = reduce_down(place, hidden, held, down_weight, total, step, last)

    down = total.astype(jnp.bfloat16).reshape(steps, count, -1)
    down_sum = lax.psum_scatter(down, "gy", scatter_dimension=1, tiled=True).astype(jnp.float32)
    return (down_sum * down_scale).astype(jnp.bfloat16)


def solution(mesh):
    placed = (
        P(None, ("groups", "gy"), "gx"),
        P("gx", "gy"),
        P("gx", "gy"),
        P("gy"),
        P("gy"),
        P("gy", "gx"),
        P("gx"),
    )
    return jax.shard_map(
        functools.partial(per_device, mesh),
        mesh=mesh,
        in_specs=placed,
        out_specs=P(None, ("groups", "gy"), "gx"),
        check_vma=False,
    )
```

time: 515 us -> 411 us (0.80)
  waiting for transfers between devices: 374 us -> 175 us
  Pallas kernels: 0 us -> 127 us
  starting transfers between devices: 0.27 us -> 86.1 us
  matrix products: 84.7 us -> 0 us
  other arithmetic: 22.5 us -> 3.27 us
  blocking collectives: 18.8 us -> 0 us
    psum x1 -> x0, waiting for transfers between devices: 352 us -> none  [block(): lax.psum(partial_terms.astype(jnp.bfloat16), 'gx').astype(jnp.float32)]
    pallas_call x0 -> x48, Pallas kernels: none -> 127 us  [the longest x16 58 us: project(): pl.pallas_call(kernel, grid_spec=pltpu.PrefetchScalarGridSpec(num_scalar_...]
    ppermute x0 -> x30, waiting for transfers between devices: none -> 121 us  [the longest x15 74.8 us: per_device(): got = lax.ppermute(send, ('gx', 'gy'), towards)]
    ppermute x0 -> x30, starting transfers between devices: none -> 86 us  [the longest x15 66.5 us: per_device(): held = lax.ppermute(passed, ('gx', 'gy'), back)]
    dot_general x6 -> x0, matrix products: 84.7 us -> none  [the longest x2 37.3 us: block(): jnp.einsum('srf,fd->srd', hidden, down_weight, preferred_element_type=jnp...]
    all_gather x0 -> x1, waiting for transfers between devices: none -> 22.4 us  [per_device(): rows = lax.all_gather(tokens, 'gy', axis=1, tiled=True)]
    all_gather x2 -> x0, blocking collectives: 18.8 us -> none  [block(): piece = lax.all_gather(rows_in, 'gy', axis=1, tiled=True)]
    convert_element_type x3 -> x2, other arithmetic: 16.3 us -> 3.21 us  [the longest x1 1.81 us: per_device(): return (down_sum * down_scale).astype(jnp.bfloat16)]
  transfers between devices with their start and end apart: 3 -> 32, of which waited for: 2 -> 23; matrix products, arithmetic and copies ran while one was open for 5% -> 0% of each run, Pallas kernels for 0% -> 25%
where the time goes in v1:
time: 411 us; the launch traced here: 409 us
  waiting for transfers between devices  175 us (43%)
  Pallas kernels  127 us (31%)
  starting transfers between devices  86.1 us (21%)
  between operations  14.1 us (3%)
    ppermute x15, waiting for transfers between devices, per_device(): got = lax.ppermute(send, ('gx', 'gy'), towards)  74.8 us
    ppermute x15, starting transfers between devices, per_device(): held = lax.ppermute(passed, ('gx', 'gy'), back)  66.5 us
    pallas_call x16, Pallas kernels, project(): pl.pallas_call(kernel, grid_spec=pltpu.PrefetchScalarGridSpec(num_scalar_...  58 us
    pallas_call x16, Pallas kernels, reduce_down(): pl.pallas_call(kernel, grid_spec=pltpu.PrefetchScalarGridSpec(num_scalar_...  54.7 us
    ppermute x15, waiting for transfers between devices, per_device(): held = lax.ppermute(passed, ('gx', 'gy'), back)  46.5 us
    reduce_scatter x1, waiting for transfers between devices, per_device(): lax.psum_scatter(down, 'gy', scatter_dimension=1, tiled=True)  30.6 us
    all_gather x1, waiting for transfers between devices, per_device(): rows = lax.all_gather(tokens, 'gy', axis=1, tiled=True)  22.4 us
    ppermute x15, starting transfers between devices, per_device(): got = lax.ppermute(send, ('gx', 'gy'), towards)  19.5 us
  transfers between devices with their start and end apart: 32, of which 23 were waited for; matrix products, arithmetic and copies ran while one was open for 0% of the time, Pallas kernels for 25%

profile of v1, /device:TPU:0, one launch (start us, length us, event | category | flops | bytes accessed | tf_op | source)
XLA Modules:
  0.0 408.8 jit_solution(15528072599531700226)
XLA Ops:
  8.9 22.4 %all-gather.2.cloned.1.call-done = bf16[2,192,2048]{2,1,0:T(8,128)(2,1)} async-done(((bf16[2,48,2048]{2,1,0:T(8,128)(2,1)}), bf16[2,192,2048]{2,1,0:T(8,128)(2,1)}) %all-gather.2.cloned.1.call-update) | async-done | bytes 1572880 | tf_op jit(solution)/shard_map/all_gather | solution.py:172
  43.0 8.9 %collective-permute-done.recv_ref = bf16[2,384,512]{2,1,0:T(8,128)(2,1)S(1)} collective-permute-done((bf16[2,384,512]{2,1,0:T(8,128)(2,1)S(1)}, bf16[2,384,512]{2,1,0:T(8,128)(2,1)S(1)}, u32[]{:S(2)}, u32[]{:S(2)}) %collective-permute-start) | collective-permute-done | bytes 786464 | tf_op jit(solution)/shard_map/ppermute | solution.py:184
  58.6 9.0 %collective-permute-done.1.recv_ref = bf16[2,384,512]{2,1,0:T(8,128)(2,1)S(1)} collective-permute-done((bf16[2,384,512]{2,1,0:T(8,128)(2,1)S(1)}, bf16[2,384,512]{2,1,0:T(8,128)(2,1)S(1)}, u32[]{:S(2)}, u32[]{:S(2)}) %collective-permute-start.1) | collective-permute-done | bytes 786464 | tf_op jit(solution)/shard_map/ppermute | solution.py:184
  74.2 9.0 %collective-permute-done.2.recv_ref = bf16[2,384,512]{2,1,0:T(8,128)(2,1)S(1)} collective-permute-done((bf16[2,384,512]{2,1,0:T(8,128)(2,1)S(1)}, bf16[2,384,512]{2,1,0:T(8,128)(2,1)S(1)}, u32[]{:S(2)}, u32[]{:S(2)}) %collective-permute-start.2) | collective-permute-done | bytes 786464 | tf_op jit(solution)/shard_map/ppermute | solution.py:184
  88.7 9.0 %collective-permute-done.3.recv_ref = bf16[2,384,512]{2,1,0:T(8,128)(2,1)S(1)} collective-permute-done((bf16[2,384,512]{2,1,0:T(8,128)(2,1)S(1)}, bf16[2,384,512]{2,1,0:T(8,128)(2,1)S(1)}, u32[]{:S(2)}, u32[]{:S(2)}) %collective-permute-start.3) | collective-permute-done | bytes 786464 | tf_op jit(solution)/shard_map/ppermute | solution.py:184
  103.2 9.0 %collective-permute-done.4.recv_ref = bf16[2,384,512]{2,1,0:T(8,128)(2,1)S(1)} collective-permute-done((bf16[2,384,512]{2,1,0:T(8,128)(2,1)S(1)}, bf16[2,384,512]{2,1,0:T(8,128)(2,1)S(1)}, u32[]{:S(2)}, u32[]{:S(2)}) %collective-permute-start.4) | collective-permute-done | bytes 786464 | tf_op jit(solution)/shard_map/ppermute | solution.py:184
  117.7 9.0 %collective-permute-done.5.recv_ref = bf16[2,384,512]{2,1,0:T(8,128)(2,1)S(1)} collective-permute-done((bf16[2,384,512]{2,1,0:T(8,128)(2,1)S(1)}, bf16[2,384,512]{2,1,0:T(8,128)(2,1)S(1)}, u32[]{:S(2)}, u32[]{:S(2)}) %collective-permute-start.5) | collective-permute-done | bytes 786464 | tf_op jit(solution)/shard_map/ppermute | solution.py:184
  132.3 9.0 %collective-permute-done.6.recv_ref = bf16[2,384,512]{2,1,0:T(8,128)(2,1)S(1)} collective-permute-done((bf16[2,384,512]{2,1,0:T(8,128)(2,1)S(1)}, bf16[2,384,512]{2,1,0:T(8,128)(2,1)S(1)}, u32[]{:S(2)}, u32[]{:S(2)}) %collective-permute-start.6) | collective-permute-done | bytes 786464 | tf_op jit(solution)/shard_map/ppermute | solution.py:184
  146.8 9.0 %collective-permute-done.7.recv_ref = bf16[2,384,512]{2,1,0:T(8,128)(2,1)S(1)} collective-permute-done((bf16[2,384,512]{2,1,0:T(8,128)(2,1)S(1)}, bf16[2,384,512]{2,1,0:T(8,128)(2,1)S(1)}, u32[]{:S(2)}, u32[]{:S(2)}) %collective-permute-start.7) | collective-permute-done | bytes 786464 | tf_op jit(solution)/shard_map/ppermute | solution.py:184
  177.9 4.4 %collective-permute-start.16 = (bf16[384,512]{1,0:T(8,128)(2,1)S(1)}, bf16[384,512]{1,0:T(8,128)(2,1)S(1)}, u32[]{:S(2)}, u32[]{:S(2)}) collective-permute-start(bf16[384,512]{1,0:T(8,128)(2,1)S(1)} %get-tuple-element.94), channel_id=1, source_target_pairs={{5,1},{7,3},{0,4},{9,5},{2,6},{11,7},{4,8},{13,9},{6,10},{15,11},{... | collective-permute-start | bytes 1179656 | tf_op jit(solution)/shard_map/ppermute | solution.py:190
  182.3 5.3 %collective-permute-done.16.recv_ref = bf16[384,512]{1,0:T(8,128)(2,1)S(1)} collective-permute-done((bf16[384,512]{1,0:T(8,128)(2,1)S(1)}, bf16[384,512]{1,0:T(8,128)(2,1)S(1)}, u32[]{:S(2)}, u32[]{:S(2)}) %collective-permute-start.16) | collective-permute-done | bytes 393248 | tf_op jit(solution)/shard_map/ppermute | solution.py:190
  191.1 4.4 %collective-permute-start.17 = (bf16[384,512]{1,0:T(8,128)(2,1)S(1)}, bf16[384,512]{1,0:T(8,128)(2,1)S(1)}, u32[]{:S(2)}, u32[]{:S(2)}) collective-permute-start(bf16[384,512]{1,0:T(8,128)(2,1)S(1)} %get-tuple-element.96), channel_id=1, source_target_pairs={{5,1},{7,3},{0,4},{9,5},{2,6},{11,7},{4,8},{13,9},{6,10},{15,11},{... | collective-permute-start | bytes 1179656 | tf_op jit(solution)/shard_map/ppermute | solution.py:190
  206.2 4.4 %collective-permute-start.18 = (bf16[384,512]{1,0:T(8,128)(2,1)S(1)}, bf16[384,512]{1,0:T(8,128)(2,1)S(1)}, u32[]{:S(2)}, u32[]{:S(2)}) collective-permute-start(bf16[384,512]{1,0:T(8,128)(2,1)S(1)} %get-tuple-element.98), channel_id=1, source_target_pairs={{5,1},{7,3},{0,4},{9,5},{2,6},{11,7},{4,8},{13,9},{6,10},{15,11},{... | collective-permute-start | bytes 1179656 | tf_op jit(solution)/shard_map/ppermute | solution.py:190
  210.6 5.3 %collective-permute-done.18.recv_ref = bf16[384,512]{1,0:T(8,128)(2,1)S(1)} collective-permute-done((bf16[384,512]{1,0:T(8,128)(2,1)S(1)}, bf16[384,512]{1,0:T(8,128)(2,1)S(1)}, u32[]{:S(2)}, u32[]{:S(2)}) %collective-permute-start.18) | collective-permute-done | bytes 393248 | tf_op jit(solution)/shard_map/ppermute | solution.py:190
  219.4 4.4 %collective-permute-start.19 = (bf16[384,512]{1,0:T(8,128)(2,1)S(1)}, bf16[384,512]{1,0:T(8,128)(2,1)S(1)}, u32[]{:S(2)}, u32[]{:S(2)}) collective-permute-start(bf16[384,512]{1,0:T(8,128)(2,1)S(1)} %get-tuple-element.100), channel_id=1, source_target_pairs={{5,1},{7,3},{0,4},{9,5},{2,6},{11,7},{4,8},{13,9},{6,10},{15,11},{... | collective-permute-start | bytes 1179656 | tf_op jit(solution)/shard_map/ppermute | solution.py:190
  233.0 4.6 %collective-permute-start.20 = (bf16[384,512]{1,0:T(8,128)(2,1)S(1)}, bf16[384,512]{1,0:T(8,128)(2,1)S(1)}, u32[]{:S(2)}, u32[]{:S(2)}) collective-permute-start(bf16[384,512]{1,0:T(8,128)(2,1)S(1)} %get-tuple-element.102), channel_id=1, source_target_pairs={{5,1},{7,3},{0,4},{9,5},{2,6},{11,7},{4,8},{13,9},{6,10},{15,11},{... | collective-permute-start | bytes 1179656 | tf_op jit(solution)/shard_map/ppermute | solution.py:190
  237.6 5.3 %collective-permute-done.20.recv_ref = bf16[384,512]{1,0:T(8,128)(2,1)S(1)} collective-permute-done((bf16[384,512]{1,0:T(8,128)(2,1)S(1)}, bf16[384,512]{1,0:T(8,128)(2,1)S(1)}, u32[]{:S(2)}, u32[]{:S(2)}) %collective-permute-start.20) | collective-permute-done | bytes 393248 | tf_op jit(solution)/shard_map/ppermute | solution.py:190
  246.4 4.4 %collective-permute-start.21 = (bf16[384,512]{1,0:T(8,128)(2,1)S(1)}, bf16[384,512]{1,0:T(8,128)(2,1)S(1)}, u32[]{:S(2)}, u32[]{:S(2)}) collective-permute-start(bf16[384,512]{1,0:T(8,128)(2,1)S(1)} %get-tuple-element.104), channel_id=1, source_target_pairs={{5,1},{7,3},{0,4},{9,5},{2,6},{11,7},{4,8},{13,9},{6,10},{15,11},{... | collective-permute-start | bytes 1179656 | tf_op jit(solution)/shard_map/ppermute | solution.py:190
  260.0 4.7 %collective-permute-start.22 = (bf16[384,512]{1,0:T(8,128)(2,1)S(1)}, bf16[384,512]{1,0:T(8,128)(2,1)S(1)}, u32[]{:S(2)}, u32[]{:S(2)}) collective-permute-start(bf16[384,512]{1,0:T(8,128)(2,1)S(1)} %get-tuple-element.106), channel_id=1, source_target_pairs={{5,1},{7,3},{0,4},{9,5},{2,6},{11,7},{4,8},{13,9},{6,10},{15,11},{... | collective-permute-start | bytes 1179656 | tf_op jit(solution)/shard_map/ppermute | solution.py:190
  264.7 5.3 %collective-permute-done.22.recv_ref = bf16[384,512]{1,0:T(8,128)(2,1)S(1)} collective-permute-done((bf16[384,512]{1,0:T(8,128)(2,1)S(1)}, bf16[384,512]{1,0:T(8,128)(2,1)S(1)}, u32[]{:S(2)}, u32[]{:S(2)}) %collective-permute-start.22) | collective-permute-done | bytes 393248 | tf_op jit(solution)/shard_map/ppermute | solution.py:190
  273.5 4.4 %collective-permute-start.23 = (bf16[384,512]{1,0:T(8,128)(2,1)S(1)}, bf16[384,512]{1,0:T(8,128)(2,1)S(1)}, u32[]{:S(2)}, u32[]{:S(2)}) collective-permute-start(bf16[384,512]{1,0:T(8,128)(2,1)S(1)} %get-tuple-element.108), channel_id=1, source_target_pairs={{5,1},{7,3},{0,4},{9,5},{2,6},{11,7},{4,8},{13,9},{6,10},{15,11},{... | collective-permute-start | bytes 1179656 | tf_op jit(solution)/shard_map/ppermute | solution.py:190
  287.8 4.4 %collective-permute-start.24 = (bf16[384,512]{1,0:T(8,128)(2,1)S(1)}, bf16[384,512]{1,0:T(8,128)(2,1)S(1)}, u32[]{:S(2)}, u32[]{:S(2)}) collective-permute-start(bf16[384,512]{1,0:T(8,128)(2,1)S(1)} %get-tuple-element.110), channel_id=1, source_target_pairs={{5,1},{7,3},{0,4},{9,5},{2,6},{11,7},{4,8},{13,9},{6,10},{15,11},{... | collective-permute-start | bytes 1179656 | tf_op jit(solution)/shard_map/ppermute | solution.py:190
  295.8 3.8 collective-permute-done.24.recv_ref
  303.2 4.4 %collective-permute-start.25 = (bf16[384,512]{1,0:T(8,128)(2,1)S(1)}, bf16[384,512]{1,0:T(8,128)(2,1)S(1)}, u32[]{:S(2)}, u32[]{:S(2)}) collective-permute-start(bf16[384,512]{1,0:T(8,128)(2,1)S(1)} %get-tuple-element.112), channel_id=1, source_target_pairs={{5,1},{7,3},{0,4},{9,5},{2,6},{11,7},{4,8},{13,9},{6,10},{15,11},{... | collective-permute-start | bytes 1179656 | tf_op jit(solution)/shard_map/ppermute | solution.py:190
  316.4 4.6 %collective-permute-start.26 = (bf16[384,512]{1,0:T(8,128)(2,1)S(1)}, bf16[384,512]{1,0:T(8,128)(2,1)S(1)}, u32[]{:S(2)}, u32[]{:S(2)}) collective-permute-start(bf16[384,512]{1,0:T(8,128)(2,1)S(1)} %get-tuple-element.114), channel_id=1, source_target_pairs={{5,1},{7,3},{0,4},{9,5},{2,6},{11,7},{4,8},{13,9},{6,10},{15,11},{... | collective-permute-start | bytes 1179656 | tf_op jit(solution)/shard_map/ppermute | solution.py:190
  330.0 4.0 collective-permute-start.27
  334.0 5.3 %collective-permute-done.27.recv_ref = bf16[384,512]{1,0:T(8,128)(2,1)S(1)} collective-permute-done((bf16[384,512]{1,0:T(8,128)(2,1)S(1)}, bf16[384,512]{1,0:T(8,128)(2,1)S(1)}, u32[]{:S(2)}, u32[]{:S(2)}) %collective-permute-start.27) | collective-permute-done | bytes 393248 | tf_op jit(solution)/shard_map/ppermute | solution.py:190
  341.9 5.3 %collective-permute-start.28 = (bf16[384,512]{1,0:T(8,128)(2,1)S(1)}, bf16[384,512]{1,0:T(8,128)(2,1)S(1)}, u32[]{:S(2)}, u32[]{:S(2)}) collective-permute-start(bf16[384,512]{1,0:T(8,128)(2,1)S(1)} %get-tuple-element.118), channel_id=1, source_target_pairs={{5,1},{7,3},{0,4},{9,5},{2,6},{11,7},{4,8},{13,9},{6,10},{15,11},{... | collective-permute-start | bytes 1179656 | tf_op jit(solution)/shard_map/ppermute | solution.py:190
  347.3 5.3 %collective-permute-done.28.recv_ref = bf16[384,512]{1,0:T(8,128)(2,1)S(1)} collective-permute-done((bf16[384,512]{1,0:T(8,128)(2,1)S(1)}, bf16[384,512]{1,0:T(8,128)(2,1)S(1)}, u32[]{:S(2)}, u32[]{:S(2)}) %collective-permute-start.28) | collective-permute-done | bytes 393248 | tf_op jit(solution)/shard_map/ppermute | solution.py:190
  355.1 4.4 %collective-permute-start.29 = (bf16[384,512]{1,0:T(8,128)(2,1)S(1)}, bf16[384,512]{1,0:T(8,128)(2,1)S(1)}, u32[]{:S(2)}, u32[]{:S(2)}) collective-permute-start(bf16[384,512]{1,0:T(8,128)(2,1)S(1)} %get-tuple-element.120), channel_id=1, source_target_pairs={{5,1},{7,3},{0,4},{9,5},{2,6},{11,7},{4,8},{13,9},{6,10},{15,11},{... | collective-permute-start | bytes 1179656 | tf_op jit(solution)/shard_map/ppermute | solution.py:190
  359.5 5.3 %collective-permute-done.29.recv_ref = bf16[384,512]{1,0:T(8,128)(2,1)S(1)} collective-permute-done((bf16[384,512]{1,0:T(8,128)(2,1)S(1)}, bf16[384,512]{1,0:T(8,128)(2,1)S(1)}, u32[]{:S(2)}, u32[]{:S(2)}) %collective-permute-start.29) | collective-permute-done | bytes 393248 | tf_op jit(solution)/shard_map/ppermute | solution.py:190
  369.5 30.6 %reduce-scatter.2.cloned.1.call-done = bf16[2,48,2048]{2,1,0:T(8,128)(2,1)} async-done(((bf16[2,192,2048]{2,1,0:T(8,128)(2,1)}), bf16[2,48,2048]{2,1,0:T(8,128)(2,1)}) %reduce-scatter.2.cloned.1.call-update) | async-done | bytes 393232 | tf_op jit(solution)/shard_map/reduce_scatter | solution.py:194
  (95 shorter events, 166.6 us)
Async XLA Ops:
  6.5 24.8 %all-gather.2.cloned.1.call-start = ((), (), s32[]{:S(2)}) async-start(), calls=%async_computation.1 | async-start | bytes 1966080 | tf_op jit(solution)/shard_map/all_gather | solution.py:172
  7.3 392.9 %reduce-scatter.2.cloned.1.call-start = ((), (), s32[]{:S(2)}) async-start(), calls=%async_computation.2 | async-start | bytes 1966080 | tf_op jit(solution)/shard_map/reduce_scatter | solution.py:194
  38.1 13.9 %collective-permute-start = (bf16[2,384,512]{2,1,0:T(8,128)(2,1)S(1)}, bf16[2,384,512]{2,1,0:T(8,128)(2,1)S(1)}, u32[]{:S(2)}, u32[]{:S(2)}) collective-permute-start(bf16[2,384,512]{2,1,0:T(8,128)(2,1)S(1)} %get-tuple-element.64), channel_id=1, source_target_pairs={{1,5},{3,7},{4,0},{5,9},{6,2},{7,11},{8,4},{9,13},{10,6},{11,15},{... | collective-permute-start | bytes 2359304 | tf_op jit(solution)/shard_map/ppermute | solution.py:184
  53.7 13.9 %collective-permute-start.1 = (bf16[2,384,512]{2,1,0:T(8,128)(2,1)S(1)}, bf16[2,384,512]{2,1,0:T(8,128)(2,1)S(1)}, u32[]{:S(2)}, u32[]{:S(2)}) collective-permute-start(bf16[2,384,512]{2,1,0:T(8,128)(2,1)S(1)} %get-tuple-element.65), channel_id=1, source_target_pairs={{1,5},{3,7},{4,0},{5,9},{6,2},{7,11},{8,4},{9,13},{10,6},{11,15},{... | collective-permute-start | bytes 2359304 | tf_op jit(solution)/shard_map/ppermute | solution.py:184
  69.3 13.9 %collective-permute-start.2 = (bf16[2,384,512]{2,1,0:T(8,128)(2,1)S(1)}, bf16[2,384,512]{2,1,0:T(8,128)(2,1)S(1)}, u32[]{:S(2)}, u32[]{:S(2)}) collective-permute-start(bf16[2,384,512]{2,1,0:T(8,128)(2,1)S(1)} %get-tuple-element.66), channel_id=1, source_target_pairs={{1,5},{3,7},{4,0},{5,9},{6,2},{7,11},{8,4},{9,13},{10,6},{11,15},{... | collective-permute-start | bytes 2359304 | tf_op jit(solution)/shard_map/ppermute | solution.py:184
  83.8 13.9 %collective-permute-start.3 = (bf16[2,384,512]{2,1,0:T(8,128)(2,1)S(1)}, bf16[2,384,512]{2,1,0:T(8,128)(2,1)S(1)}, u32[]{:S(2)}, u32[]{:S(2)}) collective-permute-start(bf16[2,384,512]{2,1,0:T(8,128)(2,1)S(1)} %get-tuple-element.67), channel_id=1, source_target_pairs={{1,5},{3,7},{4,0},{5,9},{6,2},{7,11},{8,4},{9,13},{10,6},{11,15},{... | collective-permute-start | bytes 2359304 | tf_op jit(solution)/shard_map/ppermute | solution.py:184
  98.3 13.9 %collective-permute-start.4 = (bf16[2,384,512]{2,1,0:T(8,128)(2,1)S(1)}, bf16[2,384,512]{2,1,0:T(8,128)(2,1)S(1)}, u32[]{:S(2)}, u32[]{:S(2)}) collective-permute-start(bf16[2,384,512]{2,1,0:T(8,128)(2,1)S(1)} %get-tuple-element.68), channel_id=1, source_target_pairs={{1,5},{3,7},{4,0},{5,9},{6,2},{7,11},{8,4},{9,13},{10,6},{11,15},{... | collective-permute-start | bytes 2359304 | tf_op jit(solution)/shard_map/ppermute | solution.py:184
  112.8 13.9 %collective-permute-start.5 = (bf16[2,384,512]{2,1,0:T(8,128)(2,1)S(1)}, bf16[2,384,512]{2,1,0:T(8,128)(2,1)S(1)}, u32[]{:S(2)}, u32[]{:S(2)}) collective-permute-start(bf16[2,384,512]{2,1,0:T(8,128)(2,1)S(1)} %get-tuple-element.69), channel_id=1, source_target_pairs={{1,5},{3,7},{4,0},{5,9},{6,2},{7,11},{8,4},{9,13},{10,6},{11,15},{... | collective-permute-start | bytes 2359304 | tf_op jit(solution)/shard_map/ppermute | solution.py:184
  127.3 13.9 %collective-permute-start.6 = (bf16[2,384,512]{2,1,0:T(8,128)(2,1)S(1)}, bf16[2,384,512]{2,1,0:T(8,128)(2,1)S(1)}, u32[]{:S(2)}, u32[]{:S(2)}) collective-permute-start(bf16[2,384,512]{2,1,0:T(8,128)(2,1)S(1)} %get-tuple-element.70), channel_id=1, source_target_pairs={{1,5},{3,7},{4,0},{5,9},{6,2},{7,11},{8,4},{9,13},{10,6},{11,15},{... | collective-permute-start | bytes 2359304 | tf_op jit(solution)/shard_map/ppermute | solution.py:184
  141.8 13.9 %collective-permute-start.7 = (bf16[2,384,512]{2,1,0:T(8,128)(2,1)S(1)}, bf16[2,384,512]{2,1,0:T(8,128)(2,1)S(1)}, u32[]{:S(2)}, u32[]{:S(2)}) collective-permute-start(bf16[2,384,512]{2,1,0:T(8,128)(2,1)S(1)} %get-tuple-element.71), channel_id=1, source_target_pairs={{1,5},{3,7},{4,0},{5,9},{6,2},{7,11},{8,4},{9,13},{10,6},{11,15},{... | collective-permute-start | bytes 2359304 | tf_op jit(solution)/shard_map/ppermute | solution.py:184
  156.4 15.3 %collective-permute-start.8 = (bf16[2,384,512]{2,1,0:T(8,128)(2,1)S(1)}, bf16[2,384,512]{2,1,0:T(8,128)(2,1)S(1)}, u32[]{:S(2)}, u32[]{:S(2)}) collective-permute-start(bf16[2,384,512]{2,1,0:T(8,128)(2,1)S(1)} %get-tuple-element.72), channel_id=1, source_target_pairs={{1,5},{3,7},{4,0},{5,9},{6,2},{7,11},{8,4},{9,13},{10,6},{11,15},{... | collective-permute-start | bytes 2359304 | tf_op jit(solution)/shard_map/ppermute | solution.py:184
  161.2 13.1 %collective-permute-start.15 = (bf16[384,512]{1,0:T(8,128)(2,1)S(1)}, bf16[384,512]{1,0:T(8,128)(2,1)S(1)}, u32[]{:S(2)}, u32[]{:S(2)}) collective-permute-start(bf16[384,512]{1,0:T(8,128)(2,1)S(1)} %get-tuple-element.92), channel_id=1, source_target_pairs={{5,1},{7,3},{0,4},{9,5},{2,6},{11,7},{4,8},{13,9},{6,10},{15,11},{... | collective-permute-start | bytes 1179656 | tf_op jit(solution)/shard_map/ppermute | solution.py:190
  172.3 26.8 %collective-permute-start.9 = (bf16[2,384,512]{2,1,0:T(8,128)(2,1)S(1)}, bf16[2,384,512]{2,1,0:T(8,128)(2,1)S(1)}, u32[]{:S(2)}, u32[]{:S(2)}) collective-permute-start(bf16[2,384,512]{2,1,0:T(8,128)(2,1)S(1)} %get-tuple-element.73), channel_id=1, source_target_pairs={{1,5},{3,7},{4,0},{5,9},{6,2},{7,11},{8,4},{9,13},{10,6},{11,15},{... | collective-permute-start | bytes 2359304 | tf_op jit(solution)/shard_map/ppermute | solution.py:184
  177.9 9.7 %collective-permute-start.16 = (bf16[384,512]{1,0:T(8,128)(2,1)S(1)}, bf16[384,512]{1,0:T(8,128)(2,1)S(1)}, u32[]{:S(2)}, u32[]{:S(2)}) collective-permute-start(bf16[384,512]{1,0:T(8,128)(2,1)S(1)} %get-tuple-element.94), channel_id=1, source_target_pairs={{5,1},{7,3},{0,4},{9,5},{2,6},{11,7},{4,8},{13,9},{6,10},{15,11},{... | collective-permute-start | bytes 1179656 | tf_op jit(solution)/shard_map/ppermute | solution.py:190
  191.1 11.5 %collective-permute-start.17 = (bf16[384,512]{1,0:T(8,128)(2,1)S(1)}, bf16[384,512]{1,0:T(8,128)(2,1)S(1)}, u32[]{:S(2)}, u32[]{:S(2)}) collective-permute-start(bf16[384,512]{1,0:T(8,128)(2,1)S(1)} %get-tuple-element.96), channel_id=1, source_target_pairs={{5,1},{7,3},{0,4},{9,5},{2,6},{11,7},{4,8},{13,9},{6,10},{15,11},{... | collective-permute-start | bytes 1179656 | tf_op jit(solution)/shard_map/ppermute | solution.py:190
  199.8 27.6 %collective-permute-start.10 = (bf16[2,384,512]{2,1,0:T(8,128)(2,1)S(1)}, bf16[2,384,512]{2,1,0:T(8,128)(2,1)S(1)}, u32[]{:S(2)}, u32[]{:S(2)}) collective-permute-start(bf16[2,384,512]{2,1,0:T(8,128)(2,1)S(1)} %get-tuple-element.74), channel_id=1, source_target_pairs={{1,5},{3,7},{4,0},{5,9},{6,2},{7,11},{8,4},{9,13},{10,6},{11,15},{... | collective-permute-start | bytes 2359304 | tf_op jit(solution)/shard_map/ppermute | solution.py:184
  206.2 9.7 %collective-permute-start.18 = (bf16[384,512]{1,0:T(8,128)(2,1)S(1)}, bf16[384,512]{1,0:T(8,128)(2,1)S(1)}, u32[]{:S(2)}, u32[]{:S(2)}) collective-permute-start(bf16[384,512]{1,0:T(8,128)(2,1)S(1)} %get-tuple-element.98), channel_id=1, source_target_pairs={{5,1},{7,3},{0,4},{9,5},{2,6},{11,7},{4,8},{13,9},{6,10},{15,11},{... | collective-permute-start | bytes 1179656 | tf_op jit(solution)/shard_map/ppermute | solution.py:190
  219.4 10.0 %collective-permute-start.19 = (bf16[384,512]{1,0:T(8,128)(2,1)S(1)}, bf16[384,512]{1,0:T(8,128)(2,1)S(1)}, u32[]{:S(2)}, u32[]{:S(2)}) collective-permute-start(bf16[384,512]{1,0:T(8,128)(2,1)S(1)} %get-tuple-element.100), channel_id=1, source_target_pairs={{5,1},{7,3},{0,4},{9,5},{2,6},{11,7},{4,8},{13,9},{6,10},{15,11},{... | collective-permute-start | bytes 1179656 | tf_op jit(solution)/shard_map/ppermute | solution.py:190
  228.1 26.3 %collective-permute-start.11 = (bf16[2,384,512]{2,1,0:T(8,128)(2,1)S(1)}, bf16[2,384,512]{2,1,0:T(8,128)(2,1)S(1)}, u32[]{:S(2)}, u32[]{:S(2)}) collective-permute-start(bf16[2,384,512]{2,1,0:T(8,128)(2,1)S(1)} %get-tuple-element.75), channel_id=1, source_target_pairs={{1,5},{3,7},{4,0},{5,9},{6,2},{7,11},{8,4},{9,13},{10,6},{11,15},{... | collective-permute-start | bytes 2359304 | tf_op jit(solution)/shard_map/ppermute | solution.py:184
  233.0 9.8 %collective-permute-start.20 = (bf16[384,512]{1,0:T(8,128)(2,1)S(1)}, bf16[384,512]{1,0:T(8,128)(2,1)S(1)}, u32[]{:S(2)}, u32[]{:S(2)}) collective-permute-start(bf16[384,512]{1,0:T(8,128)(2,1)S(1)} %get-tuple-element.102), channel_id=1, source_target_pairs={{5,1},{7,3},{0,4},{9,5},{2,6},{11,7},{4,8},{13,9},{6,10},{15,11},{... | collective-permute-start | bytes 1179656 | tf_op jit(solution)/shard_map/ppermute | solution.py:190
  246.4 10.0 %collective-permute-start.21 = (bf16[384,512]{1,0:T(8,128)(2,1)S(1)}, bf16[384,512]{1,0:T(8,128)(2,1)S(1)}, u32[]{:S(2)}, u32[]{:S(2)}) collective-permute-start(bf16[384,512]{1,0:T(8,128)(2,1)S(1)} %get-tuple-element.104), channel_id=1, source_target_pairs={{5,1},{7,3},{0,4},{9,5},{2,6},{11,7},{4,8},{13,9},{6,10},{15,11},{... | collective-permute-start | bytes 1179656 | tf_op jit(solution)/shard_map/ppermute | solution.py:190
  255.1 26.5 %collective-permute-start.12 = (bf16[2,384,512]{2,1,0:T(8,128)(2,1)S(1)}, bf16[2,384,512]{2,1,0:T(8,128)(2,1)S(1)}, u32[]{:S(2)}, u32[]{:S(2)}) collective-permute-start(bf16[2,384,512]{2,1,0:T(8,128)(2,1)S(1)} %get-tuple-element.76), channel_id=1, source_target_pairs={{1,5},{3,7},{4,0},{5,9},{6,2},{7,11},{8,4},{9,13},{10,6},{11,15},{... | collective-permute-start | bytes 2359304 | tf_op jit(solution)/shard_map/ppermute | solution.py:184
  260.0 9.9 %collective-permute-start.22 = (bf16[384,512]{1,0:T(8,128)(2,1)S(1)}, bf16[384,512]{1,0:T(8,128)(2,1)S(1)}, u32[]{:S(2)}, u32[]{:S(2)}) collective-permute-start(bf16[384,512]{1,0:T(8,128)(2,1)S(1)} %get-tuple-element.106), channel_id=1, source_target_pairs={{5,1},{7,3},{0,4},{9,5},{2,6},{11,7},{4,8},{13,9},{6,10},{15,11},{... | collective-permute-start | bytes 1179656 | tf_op jit(solution)/shard_map/ppermute | solution.py:190
  273.5 10.7 %collective-permute-start.23 = (bf16[384,512]{1,0:T(8,128)(2,1)S(1)}, bf16[384,512]{1,0:T(8,128)(2,1)S(1)}, u32[]{:S(2)}, u32[]{:S(2)}) collective-permute-start(bf16[384,512]{1,0:T(8,128)(2,1)S(1)} %get-tuple-element.108), channel_id=1, source_target_pairs={{5,1},{7,3},{0,4},{9,5},{2,6},{11,7},{4,8},{13,9},{6,10},{15,11},{... | collective-permute-start | bytes 1179656 | tf_op jit(solution)/shard_map/ppermute | solution.py:190
  282.2 25.3 %collective-permute-start.13 = (bf16[2,384,512]{2,1,0:T(8,128)(2,1)S(1)}, bf16[2,384,512]{2,1,0:T(8,128)(2,1)S(1)}, u32[]{:S(2)}, u32[]{:S(2)}) collective-permute-start(bf16[2,384,512]{2,1,0:T(8,128)(2,1)S(1)} %get-tuple-element.77), channel_id=1, source_target_pairs={{1,5},{3,7},{4,0},{5,9},{6,2},{7,11},{8,4},{9,13},{10,6},{11,15},{... | collective-permute-start | bytes 2359304 | tf_op jit(solution)/shard_map/ppermute | solution.py:184
  287.8 11.8 %collective-permute-start.24 = (bf16[384,512]{1,0:T(8,128)(2,1)S(1)}, bf16[384,512]{1,0:T(8,128)(2,1)S(1)}, u32[]{:S(2)}, u32[]{:S(2)}) collective-permute-start(bf16[384,512]{1,0:T(8,128)(2,1)S(1)} %get-tuple-element.110), channel_id=1, source_target_pairs={{5,1},{7,3},{0,4},{9,5},{2,6},{11,7},{4,8},{13,9},{6,10},{15,11},{... | collective-permute-start | bytes 1179656 | tf_op jit(solution)/shard_map/ppermute | solution.py:190
  303.2 9.7 %collective-permute-start.25 = (bf16[384,512]{1,0:T(8,128)(2,1)S(1)}, bf16[384,512]{1,0:T(8,128)(2,1)S(1)}, u32[]{:S(2)}, u32[]{:S(2)}) collective-permute-start(bf16[384,512]{1,0:T(8,128)(2,1)S(1)} %get-tuple-element.112), channel_id=1, source_target_pairs={{5,1},{7,3},{0,4},{9,5},{2,6},{11,7},{4,8},{13,9},{6,10},{15,11},{... | collective-permute-start | bytes 1179656 | tf_op jit(solution)/shard_map/ppermute | solution.py:190
  308.2 16.4 %collective-permute-start.14 = (bf16[2,384,512]{2,1,0:T(8,128)(2,1)S(1)}, bf16[2,384,512]{2,1,0:T(8,128)(2,1)S(1)}, u32[]{:S(2)}, u32[]{:S(2)}) collective-permute-start(bf16[2,384,512]{2,1,0:T(8,128)(2,1)S(1)} %get-tuple-element.78), channel_id=1, source_target_pairs={{1,5},{3,7},{4,0},{5,9},{6,2},{7,11},{8,4},{9,13},{10,6},{11,15},{... | collective-permute-start | bytes 2359304 | tf_op jit(solution)/shard_map/ppermute | solution.py:184
  316.4 10.0 %collective-permute-start.26 = (bf16[384,512]{1,0:T(8,128)(2,1)S(1)}, bf16[384,512]{1,0:T(8,128)(2,1)S(1)}, u32[]{:S(2)}, u32[]{:S(2)}) collective-permute-start(bf16[384,512]{1,0:T(8,128)(2,1)S(1)} %get-tuple-element.114), channel_id=1, source_target_pairs={{5,1},{7,3},{0,4},{9,5},{2,6},{11,7},{4,8},{13,9},{6,10},{15,11},{... | collective-permute-start | bytes 1179656 | tf_op jit(solution)/shard_map/ppermute | solution.py:190
  330.0 9.3 %collective-permute-start.27 = (bf16[384,512]{1,0:T(8,128)(2,1)S(1)}, bf16[384,512]{1,0:T(8,128)(2,1)S(1)}, u32[]{:S(2)}, u32[]{:S(2)}) collective-permute-start(bf16[384,512]{1,0:T(8,128)(2,1)S(1)} %get-tuple-element.116), channel_id=1, source_target_pairs={{5,1},{7,3},{0,4},{9,5},{2,6},{11,7},{4,8},{13,9},{6,10},{15,11},{... | collective-permute-start | bytes 1179656 | tf_op jit(solution)/shard_map/ppermute | solution.py:190
  341.9 10.6 %collective-permute-start.28 = (bf16[384,512]{1,0:T(8,128)(2,1)S(1)}, bf16[384,512]{1,0:T(8,128)(2,1)S(1)}, u32[]{:S(2)}, u32[]{:S(2)}) collective-permute-start(bf16[384,512]{1,0:T(8,128)(2,1)S(1)} %get-tuple-element.118), channel_id=1, source_target_pairs={{5,1},{7,3},{0,4},{9,5},{2,6},{11,7},{4,8},{13,9},{6,10},{15,11},{... | collective-permute-start | bytes 1179656 | tf_op jit(solution)/shard_map/ppermute | solution.py:190
  355.1 9.7 %collective-permute-start.29 = (bf16[384,512]{1,0:T(8,128)(2,1)S(1)}, bf16[384,512]{1,0:T(8,128)(2,1)S(1)}, u32[]{:S(2)}, u32[]{:S(2)}) collective-permute-start(bf16[384,512]{1,0:T(8,128)(2,1)S(1)} %get-tuple-element.120), channel_id=1, source_target_pairs={{5,1},{7,3},{0,4},{9,5},{2,6},{11,7},{4,8},{13,9},{6,10},{15,11},{... | collective-permute-start | bytes 1179656 | tf_op jit(solution)/shard_map/ppermute | solution.py:190
  (3 other events, 36.5 us)
Sparse Core Ops, SparseCore 0:
  8.9 22.3 all-gather.1
  369.6 30.4 reduce-scatter.1
